TPU v7x, 32 devices: a whole 2x2x4 slice. The times are simulated.
32 devices in a mesh: groups: 2 (over x), gx: 16 (over z, y, core).
Axes of the slice: x: 2, y: 2, z: 4, core: 2. Of those that a mesh axis runs over, the one named last changes fastest.
Arguments:
- cotangent: float32 [16, 2048, 2048], P('groups', 'gx'), parts along dimension 0, may hold values from -6 to 6
- saved_v: float32 [16, 2048, 2048], P('groups', 'gx'), parts along dimension 0, may hold values from 0.3 to 3
- saved_u: float32 [16, 2048, 2048], P('groups', None, 'gx'), parts along dimension 0, may hold values from 0.3 to 3
- gain_x: float32 [2048], replicated, may hold values from 0.1 to 1.9
- width_x: int32 [2048], replicated, may hold values from 16 to 256
- gain_y: float32 [2048], replicated, may hold values from 0.1 to 1.9
- width_y: int32 [2048], replicated, may hold values from 16 to 256
Outputs:
- grad_u: float32 [16, 2048, 2048], P('groups', None, 'gx'), parts along dimension 0
- grad_v: float32 [16, 2048, 2048], P('groups', 'gx'), parts along dimension 0
There are 2 independent parts, one for each index of `groups`. A program takes and returns all parts, laid end to end along the dimension named above; an argument that names none is the same for every part. Nothing has to cross between parts.
All inputs are finite; a program needn't handle non-finite values.
Results may differ from a plain program's by a relative error of at most 0.00007.
Values sent between devices are 32-bit elements; how exact they have to be, the bound alone decides.
A program may use at most 192 MiB of HBM per device.

v0:
```python
import math

import jax
import jax.numpy as jnp
from jax import lax
from jax.sharding import PartitionSpec as P

SIGMA = 64


def build_kernel(gain, width, count):
    rows = jnp.arange(count, dtype=jnp.int32)[:, None]
    cols = jnp.arange(count, dtype=jnp.int32)[None, :]
    offset = (rows - cols).astype(jnp.float32)
    scale = 1.0 / math.sqrt(SIGMA * math.sqrt(math.pi))
    values = gain[:, None] * jnp.exp(-offset * offset / (2.0 * SIGMA * SIGMA)) * scale
    cutoff = jnp.minimum(width[:, None], width[None, :])
    return jnp.where(jnp.abs(rows - cols) <= cutoff, values, jnp.zeros_like(values))


def on_device(cotangent, saved_v, saved_u, gain_x, width_x, gain_y, width_y):
    kernel_x = build_kernel(gain_x, width_x, gain_x.shape[0])
    kernel_y = build_kernel(gain_y, width_y, gain_y.shape[0])
    high = lax.Precision.HIGHEST

    def smooth_x(field):
        return jnp.einsum("ziy,ij->zjy", field, kernel_x, precision=high)

    def smooth_y(field):
        return jnp.einsum("zxi,ij->zxj", field, kernel_y, precision=high)

    weighted = saved_v * cotangent
    along_y = smooth_y(weighted)
    middle = smooth_x(lax.all_to_all(along_y, "gx", split_axis=2, concat_axis=1, tiled=True))
    grad_u = saved_u * middle
    back_x = smooth_x(grad_u)
    grad_v = smooth_y(lax.all_to_all(back_x, "gx", split_axis=1, concat_axis=2, tiled=True))
    return (grad_u, grad_v)


def solution(mesh):
    in_specs = (
        P("groups", "gx", None),
        P("groups", "gx", None),
        P("groups", None, "gx"),
        P(),
        P(),
        P(),
        P(),
    )
    out_specs = (P("groups", None, "gx"), P("groups", "gx", None))
    return jax.shard_map(
        on_device, mesh=mesh, in_specs=in_specs, out_specs=out_specs, check_vma=False
    )
```

profile of v0, /device:TPU:13, one launch (start us, length us, event | category | flops | bytes accessed | tf_op | source)
XLA Modules:
  0.0 777.6 jit_solution(17651550982807790760)
XLA Ops:
  0.6 0.0 copy-start.4
  0.6 0.0 copy-start.3
  0.7 11.9 %fusion.73 = f32[8,128,2048]{2,1,0:T(8,128)} fusion(f32[8,128,2048]{2,1,0:T(8,128)} %param.8, f32[8,128,2048]{2,1,0:T(8,128)} %param.7), kind=kLoop, calls=%fused_computation.25.clone.2 | loop fusion | flops 2097152 | bytes 25165824 | tf_op jit(solution)/shard_map/zxi,ij->zxj/dot_general | solution.py:30
  12.5 0.0 copy-done.4
  12.5 0.0 copy-done.3
  12.5 86.6 %fusion.4 = f32[8,128,2048]{2,1,0:T(8,128)} fusion(f32[2048]{0:T(1024)S(1)} %copy-done.4, s32[2048]{0:T(1024)S(1)} %copy-done.3, f32[8,128,2048]{2,1,0:T(8,128)} %fusion.73), kind=kOutput, calls=%fused_computation.5 | convolution fusion | flops 51585744896 | bytes 16793600 | tf_op jit(solution)/shard_map/zxi,ij->zxj/dot_general | solution.py:30
  99.2 9.3 %copy.13 = f32[8,128,2048]{1,0,2:T(8,128)} copy(f32[8,128,2048]{2,1,0:T(8,128)} %fusion.4) | data formatting | bytes 16777216 | tf_op jit(solution)/shard_map/zxi,ij->zxj/dot_general | solution.py:30
  108.4 6.6 all-to-all-start
  115.0 0.0 copy-done.1
  115.0 0.0 copy-done.2
  115.0 12.5 %fusion.75 = f32[2048,2048,1]{1,0,2:T(8,128)} fusion(f32[2048]{0:T(1024)S(1)} %copy-done.2, s32[2048]{0:T(1024)S(1)} %copy-done.1), kind=kLoop, calls=%fused_computation.10.clone.clone.clone.1 | loop fusion | flops 46137344 | bytes 16793600 | tf_op jit(solution)/shard_map/ziy,ij->zjy/dot_general | solution.py:27
  127.5 12.4 %fusion.77 = f32[2048,2048,1]{1,0,2:T(8,128)} fusion(f32[2048]{0:T(1024)S(1)} %copy-done.2, s32[2048]{0:T(1024)S(1)} %copy-done.1), kind=kLoop, calls=%fused_computation.8.clone.clone.clone.1 | loop fusion | flops 46137344 | bytes 16793600 | tf_op jit(solution)/shard_map/ziy,ij->zjy/dot_general | solution.py:27
  139.9 157.4 %all-to-all-done = f32[8,128,2048]{1,0,2:T(8,128)} async-done(((f32[8,128,2048]{1,0,2:T(8,128)}), f32[8,128,2048]{1,0,2:T(8,128)}, u32[]{:S(2)}, u32[]{:S(2)}) %all-to-all-start) | async-done | bytes 8388640 | tf_op jit(solution)/shard_map/all_to_all | solution.py:34
  297.3 9.3 %copy.14 = f32[8,128,16,128]{3,1,2,0:T(8,128)} copy(f32[8,128,16,128]{1,0,3,2:T(8,128)} %bitcast.2) | data formatting | bytes 16777216 | tf_op jit(solution)/shard_map/all_to_all | solution.py:34
  306.6 71.0 %bitcast_multiply_fusion = f32[8,2048,128]{2,1,0:T(8,128)} fusion(f32[8,2048,128]{2,1,0:T(8,128)} %param.9, f32[8,2048,128]{2,1,0:T(8,128)} %bitcast.54, f32[2048,2048,1]{1,0,2:T(8,128)} %fusion.75), kind=kOutput, calls=%fused_computation.17 | convolution fusion | flops 51541704704 | bytes 41943040 | tf_op jit(solution)/shard_map/ziy,ij->zjy/dot_general | solution.py:27
  377.6 0.0 copy-done
  377.6 112.4 %fusion.38 = f32[8,2048,128]{2,1,0:T(8,128)} fusion(f32[8,2048,128]{2,1,0:T(8,128)} %bitcast_multiply_fusion, f32[2048,2048,1]{1,0,2:T(8,128)S(1)} %copy-done), kind=kOutput, calls=%fused_computation.44 | convolution fusion | flops 51539607552 | bytes 33554432 | tf_op jit(solution)/shard_map/ziy,ij->zjy/dot_general | solution.py:27
  490.0 10.6 %copy.17 = f32[8,2048,128]{2,0,1:T(8,128)} copy(f32[8,2048,128]{2,1,0:T(8,128)} %fusion.38) | data formatting | bytes 16777216 | tf_op jit(solution)/shard_map/ziy,ij->zjy/transpose | solution.py:27
  500.6 4.9 all-to-all-start.1
  505.6 12.5 %fusion.71 = f32[2048,2048,1]{1,0,2:T(8,128)} fusion(f32[2048]{0:T(1024)S(1)} %copy-done.4, s32[2048]{0:T(1024)S(1)} %copy-done.3), kind=kLoop, calls=%fused_computation.4.clone.1 | loop fusion | flops 46137344 | bytes 16793600 | tf_op jit(solution)/shard_map/zxi,ij->zxj/dot_general | solution.py:30
  518.0 169.9 %all-to-all-done.1 = f32[8,2048,128]{2,0,1:T(8,128)} async-done(((f32[8,2048,128]{2,0,1:T(8,128)}), f32[8,2048,128]{2,0,1:T(8,128)}, u32[]{:S(2)}, u32[]{:S(2)}) %all-to-all-start.1) | async-done | bytes 8388640 | tf_op jit(solution)/shard_map/all_to_all | solution.py:37
  687.9 11.6 %copy.24 = f32[8,16,128,128]{3,1,2,0:T(8,128)} copy(f32[8,16,128,128]{3,0,2,1:T(8,128)} %bitcast.8) | data formatting | bytes 16777216 | tf_op jit(solution)/shard_map/all_to_all | solution.py:37
  699.5 9.3 %all_to_all.33 = f32[8,128,2048]{2,1,0:T(8,128)} reshape(f32[8,128,16,128]{3,2,1,0:T(8,128)} %bitcast.53) | data formatting | bytes 16777216 | tf_op jit(solution)/shard_map/all_to_all | solution.py:37
  708.8 68.4 %fusion.2 = f32[8,128,2048]{2,1,0:T(8,128)} fusion(f32[8,128,2048]{2,1,0:T(8,128)} %all_to_all.33, f32[2048,2048,1]{1,0,2:T(8,128)} %fusion.71), kind=kOutput, calls=%fused_computation.3 | convolution fusion | flops 51539607552 | bytes 33554432 | tf_op jit(solution)/shard_map/zxi,ij->zxj/dot_general | solution.py:30
  (3 shorter events, 0.0 us)
Async XLA Ops:
  0.6 11.9 %copy-start.4 = (f32[2048]{0:T(1024)S(1)}, f32[2048]{0:T(1024)}, u32[]{:S(2)}) copy-start(f32[2048]{0:T(1024)} %param.12) | copy-start | bytes 24580
  0.6 11.9 %copy-start.3 = (s32[2048]{0:T(1024)S(1)}, s32[2048]{0:T(1024)}, u32[]{:S(2)}) copy-start(s32[2048]{0:T(1024)} %param.13) | copy-start | bytes 24580
  99.2 15.8 %copy-start.1 = (s32[2048]{0:T(1024)S(1)}, s32[2048]{0:T(1024)}, u32[]{:S(2)}) copy-start(s32[2048]{0:T(1024)} %param.11) | copy-start | bytes 24580
  99.2 15.9 %copy-start.2 = (f32[2048]{0:T(1024)S(1)}, f32[2048]{0:T(1024)}, u32[]{:S(2)}) copy-start(f32[2048]{0:T(1024)} %param.10) | copy-start | bytes 24580
  108.4 188.9 %all-to-all-start = ((f32[8,128,2048]{1,0,2:T(8,128)}), f32[8,128,2048]{1,0,2:T(8,128)}, u32[]{:S(2)}, u32[]{:S(2)}) async-start(f32[8,128,2048]{1,0,2:T(8,128)} %copy.13), calls=%async_computation | async-start | bytes 16777216 | tf_op jit(solution)/shard_map/all_to_all | solution.py:34
  306.6 71.0 %copy-start = (f32[2048,2048,1]{1,0,2:T(8,128)S(1)}, f32[2048,2048,1]{1,0,2:T(8,128)}, u32[]{:S(2)}) copy-start(f32[2048,2048,1]{1,0,2:T(8,128)} %fusion.77) | copy-start | bytes 50331652
  500.6 187.3 %all-to-all-start.1 = ((f32[8,2048,128]{2,0,1:T(8,128)}), f32[8,2048,128]{2,0,1:T(8,128)}, u32[]{:S(2)}, u32[]{:S(2)}) async-start(f32[8,2048,128]{2,0,1:T(8,128)} %copy.17), calls=%async_computation.1 | async-start | bytes 16777216 | tf_op jit(solution)/shard_map/all_to_all | solution.py:37
where the time goes:
time: 786 us; the launch traced here: 778 us
  matrix products  338 us (43%)
  waiting for transfers between devices  327 us (42%)
  local copies, waits for them, and re-layouts  50.1 us (6%)
  other arithmetic  49.2 us (6%)
  starting transfers between devices  11.5 us (1%)
    dot_general x2, matrix products, smooth_x(): return jnp.einsum('ziy,ij->zjy', field, kernel_x, precision=high)  183 us
    all_to_all x1, waiting for transfers between devices, on_device(): lax.all_to_all(back_x, 'gx', split_axis=1, concat_axis=2, tiled=True)  170 us
    all_to_all x1, waiting for transfers between devices, on_device(): lax.all_to_all(along_y, 'gx', split_axis=2, concat_axis=1, tiled=True)  157 us
    dot_general x2, matrix products, smooth_y(): return jnp.einsum('zxi,ij->zxj', field, kernel_y, precision=high)  155 us
    dot_general x2, other arithmetic, smooth_x(): return jnp.einsum('ziy,ij->zjy', field, kernel_x, precision=high)  24.9 us
    dot_general x2, other arithmetic, smooth_y(): return jnp.einsum('zxi,ij->zxj', field, kernel_y, precision=high)  24.3 us
    all_to_all x2, local copies, waits for them, and re-layouts, on_device(): lax.all_to_all(back_x, 'gx', split_axis=1, concat_axis=2, tiled=True)  20.9 us
  transfers between devices with their start and end apart: 2, of which 2 were waited for; matrix products, arithmetic and copies ran while one was open for 5% of the time, Pallas kernels for 0%

commit v1 on v0

v1 whole, which is shorter than its diff:
```python
import functools
import math

import jax
import jax.numpy as jnp
from jax import lax
from jax.experimental import pallas as pl
from jax.experimental.pallas import tpu as pltpu
from jax.sharding import PartitionSpec as P

SIGMA = 64
REACH = 256
TILE = 256
BAND = TILE + 2 * REACH
SCALE = 1.0 / math.sqrt(SIGMA * math.sqrt(math.pi))
MESH = pl.DeviceIdType.MESH


def build_kernel(gain, width, count):
    rows = jnp.arange(count, dtype=jnp.int32)[:, None]
    cols = jnp.arange(count, dtype=jnp.int32)[None, :]
    offset = (rows - cols).astype(jnp.float32)
    values = gain[:, None] * jnp.exp(-offset * offset / (2.0 * SIGMA * SIGMA)) * SCALE
    cutoff = jnp.minimum(width[:, None], width[None, :])
    return jnp.where(jnp.abs(rows - cols) <= cutoff, values, jnp.zeros_like(values))


def plain_form(cotangent, saved_v, saved_u, gain_x, width_x, gain_y, width_y):
    kernel_x = build_kernel(gain_x, width_x, gain_x.shape[0])
    kernel_y = build_kernel(gain_y, width_y, gain_y.shape[0])
    high = lax.Precision.HIGHEST

    def smooth_x(field):
        return jnp.einsum("ziy,ij->zjy", field, kernel_x, precision=high)

    def smooth_y(field):
        return jnp.einsum("zxi,ij->zxj", field, kernel_y, precision=high)

    weighted = saved_v * cotangent
    along_y = smooth_y(weighted)
    middle = smooth_x(lax.all_to_all(along_y, "gx", split_axis=2, concat_axis=1, tiled=True))
    grad_u = saved_u * middle
    back_x = smooth_x(grad_u)
    grad_v = smooth_y(lax.all_to_all(back_x, "gx", split_axis=1, concat_axis=2, tiled=True))
    return (grad_u, grad_v)


def parts_of(value):
    high = value.astype(jnp.bfloat16)
    return high, (value - high.astype(jnp.float32)).astype(jnp.bfloat16)


def dot(a, b):
    return jnp.dot(a, b, preferred_element_type=jnp.float32)


def three(a_hi, a_lo, b_hi, b_lo):
    return dot(a_hi, b_hi) + dot(a_hi, b_lo) + dot(a_lo, b_hi)


def fused(n, cot, sv, su, rows, cols, gu, gv,
          send_a, recv_a, send_b, recv_b, sv_buf, ky_hi, ky_lo, kx_hi, kx_lo,
          wide_hi, wide_lo, tall_hi, tall_lo,
          cot_sem, sv_sem, su_sem, gu_sem, gv_sem, sa_sem, ra_sem, sb_sem, rb_sem):
    count, mine_x, size_y = cot.shape
    size_x, mine_y = su.shape[1], su.shape[2]
    tiles_x, tiles_y = size_x // TILE, size_y // TILE
    me = lax.axis_index("gx")
    my_x = pl.multiple_of(me * mine_x, mine_x)
    my_y = pl.multiple_of(me * mine_y, mine_y)

    def load_cot(c):
        return pltpu.make_async_copy(cot.at[c], send_a.at[c], cot_sem.at[c])

    def load_sv(c):
        return pltpu.make_async_copy(sv.at[c], sv_buf.at[lax.rem(c, 2)], sv_sem.at[c])

    def load_su(c):
        return pltpu.make_async_copy(su.at[c], send_b.at[c], su_sem.at[c])

    def store_gu(c):
        return pltpu.make_async_copy(recv_a.at[c], gu.at[c], gu_sem.at[c])

    def store_gv(c):
        return pltpu.make_async_copy(send_a.at[c], gv.at[c], gv_sem.at[c])

    for c in range(count):
        load_cot(c).start()
        if c < 2:
            load_sv(c).start()

    barrier = pltpu.get_barrier_semaphore()
    for k in range(1, n):
        pl.semaphore_signal(barrier, inc=1, device_id={"gx": lax.rem(me + k, n)}, device_id_type=MESH)

    def band_start(t, size):
        return pl.multiple_of(jnp.clip(t * TILE - REACH, 0, size - BAND), TILE)

    def values(i, j, gain, width_i, width_j):
        offset = (i - j).astype(jnp.float32)
        cell = gain * jnp.exp(-offset * offset / (2.0 * SIGMA * SIGMA)) * SCALE
        return jnp.where(jnp.abs(offset) <= jnp.minimum(width_i, width_j), cell, 0.0)

    def build_y(t, _):
        i0, j0 = band_start(t, size_y), pl.multiple_of(t * TILE, TILE)
        j = j0 + lax.broadcasted_iota(jnp.int32, (TILE, TILE), 1)
        for s in range(BAND // TILE):
            at = pl.multiple_of(i0 + s * TILE, TILE)
            i = at + lax.broadcasted_iota(jnp.int32, (TILE, TILE), 0)
            hi, lo = parts_of(values(i, j, cols[pl.ds(at, TILE), 2:3], cols[pl.ds(at, TILE), 3:4],
                                     rows[3:4, pl.ds(j0, TILE)]))
            ky_hi[t, s * TILE:(s + 1) * TILE, :] = hi
            ky_lo[t, s * TILE:(s + 1) * TILE, :] = lo
        return 0

    def build_x(t, _):
        i0, j0 = band_start(t, size_x), pl.multiple_of(t * TILE, TILE)
        j = j0 + lax.broadcasted_iota(jnp.int32, (TILE, TILE), 0)
        for s in range(BAND // TILE):
            at = pl.multiple_of(i0 + s * TILE, TILE)
            i = at + lax.broadcasted_iota(jnp.int32, (TILE, TILE), 1)
            hi, lo = parts_of(values(i, j, rows[0:1, pl.ds(at, TILE)], rows[1:2, pl.ds(at, TILE)],
                                     cols[pl.ds(j0, TILE), 1:2]))
            kx_hi[t, :, s * TILE:(s + 1) * TILE] = hi
            kx_lo[t, :, s * TILE:(s + 1) * TILE] = lo
        return 0

    def smooth_y(c):
        def tile(t, _):
            band = pl.ds(band_start(t, size_y), BAND)
            send_a[c, :, pl.ds(pl.multiple_of(t * TILE, TILE), TILE)] = three(
                wide_hi[:, band], wide_lo[:, band], ky_hi[t], ky_lo[t])
            return 0
        lax.fori_loop(0, tiles_y, tile, 0)

    def smooth_x(t):
        band = pl.ds(band_start(t, size_x), BAND)
        return three(kx_hi[t], kx_lo[t], tall_hi[band, :], tall_lo[band, :])

    lax.fori_loop(0, tiles_y, build_y, 0)
    pl.semaphore_wait(barrier, n - 1)

    def first(c, _):
        load_cot(c).wait()
        load_sv(c).wait()
        hi, lo = parts_of(send_a[c] * sv_buf[lax.rem(c, 2)])
        wide_hi[...] = hi
        wide_lo[...] = lo

        @pl.when(c + 2 < count)
        def _():
            load_sv(c + 2).start()

        smooth_y(c)
        for k in range(1, n):
            p = lax.rem(me + k, n)
            pltpu.make_async_remote_copy(
                src_ref=send_a.at[c, :, pl.ds(pl.multiple_of(p * mine_y, mine_y), mine_y)],
                dst_ref=recv_a.at[c, pl.ds(my_x, mine_x), :],
                send_sem=sa_sem.at[c], recv_sem=ra_sem.at[c],
                device_id={"gx": p}, device_id_type=MESH).start()
        recv_a[c, pl.ds(my_x, mine_x), :] = send_a[c, :, pl.ds(my_y, mine_y)]
        load_su(c).start()
        return 0

    lax.fori_loop(0, count, first, 0)
    lax.fori_loop(0, tiles_x, build_x, 0)

    def tall_part(ref, c, sem):
        part = ref.at[c, pl.ds(0, size_x - mine_x), :]
        return pltpu.make_async_copy(part, part, sem.at[c])

    def wide_part(ref, c, sem):
        part = ref.at[c, :, pl.ds(0, size_y - mine_y)]
        return pltpu.make_async_copy(part, part, sem.at[c])

    def second(c, _):
        tall_part(recv_a, c, ra_sem).wait()
        hi, lo = parts_of(recv_a[c])
        tall_hi[...] = hi
        tall_lo[...] = lo
        load_su(c).wait()

        def up(t, _):
            out = pl.ds(pl.multiple_of(t * TILE, TILE), TILE)
            recv_a[c, out, :] = send_b[c, out, :] * smooth_x(t)
            return 0

        lax.fori_loop(0, tiles_x, up, 0)
        store_gu(c).start()
        hi, lo = parts_of(recv_a[c])
        tall_hi[...] = hi
        tall_lo[...] = lo

        def back(t, _):
            send_b[c, pl.ds(pl.multiple_of(t * TILE, TILE), TILE), :] = smooth_x(t)
            return 0

        lax.fori_loop(0, tiles_x, back, 0)
        for k in range(1, n):
            p = lax.rem(me + k, n)
            pltpu.make_async_remote_copy(
                src_ref=send_b.at[c, pl.ds(pl.multiple_of(p * mine_x, mine_x), mine_x), :],
                dst_ref=recv_b.at[c, :, pl.ds(my_y, mine_y)],
                send_sem=sb_sem.at[c], recv_sem=rb_sem.at[c],
                device_id={"gx": p}, device_id_type=MESH).start()
        recv_b[c, :, pl.ds(my_y, mine_y)] = send_b[c, pl.ds(my_x, mine_x), :]
        return 0

    lax.fori_loop(0, count, second, 0)

    def third(c, _):
        wide_part(send_a, c, sa_sem).wait()
        wide_part(recv_b, c, rb_sem).wait()
        hi, lo = parts_of(recv_b[c])
        wide_hi[...] = hi
        wide_lo[...] = lo
        smooth_y(c)
        store_gv(c).start()
        return 0

    lax.fori_loop(0, count, third, 0)

    def finish(c, _):
        tall_part(send_b, c, sb_sem).wait()
        store_gu(c).wait()
        store_gv(c).wait()
        return 0

    lax.fori_loop(0, count, finish, 0)


def kernel_form(n, cotangent, saved_v, saved_u, gain_x, width_x, gain_y, width_y):
    count, mine_x, size_y = cotangent.shape
    size_x, mine_y = saved_u.shape[1:]
    rows = jnp.stack([gain_x, width_x.astype(jnp.float32), gain_y, width_y.astype(jnp.float32)])
    f32, bf16 = jnp.float32, jnp.bfloat16
    work = 12 * 2 * count * BAND * (mine_x * size_y + mine_y * size_x)
    return pl.pallas_call(
        functools.partial(fused, n),
        out_shape=(jax.ShapeDtypeStruct(saved_u.shape, f32), jax.ShapeDtypeStruct(cotangent.shape, f32)),
        in_specs=[pl.BlockSpec(memory_space=pl.ANY)] * 3 + [pl.BlockSpec(memory_space=pltpu.VMEM)] * 2,
        out_specs=(pl.BlockSpec(memory_space=pl.ANY),) * 2,
        scratch_shapes=[
            pltpu.VMEM((count, mine_x, size_y), f32),
            pltpu.VMEM((count, size_x, mine_y), f32),
            pltpu.VMEM((count, size_x, mine_y), f32),
            pltpu.VMEM((count, mine_x, size_y), f32),
            pltpu.VMEM((2, mine_x, size_y), f32),
            pltpu.VMEM((size_y // TILE, BAND, TILE), bf16),
            pltpu.VMEM((size_y // TILE, BAND, TILE), bf16),
            pltpu.VMEM((size_x // TILE, TILE, BAND), bf16),
            pltpu.VMEM((size_x // TILE, TILE, BAND), bf16),
            pltpu.VMEM((mine_x, size_y), bf16),
            pltpu.VMEM((mine_x, size_y), bf16),
            pltpu.VMEM((size_x, mine_y), bf16),
            pltpu.VMEM((size_x, mine_y), bf16),
        ] + [pltpu.SemaphoreType.DMA((count,))] * 9,
        compiler_params=pltpu.CompilerParams(
            collective_id=0, has_side_effects=True, vmem_limit_bytes=60 * 2**20),
        cost_estimate=pl.CostEstimate(
            flops=work, bytes_accessed=20 * cotangent.size, transcendentals=0),
    )(cotangent, saved_v, saved_u, rows, rows.T)


def on_device(n, *arrays):
    size_y, (size_x, mine_y), mine_x = arrays[0].shape[2], arrays[2].shape[1:], arrays[0].shape[1]
    fits = (size_x % TILE == 0 and size_y % TILE == 0 and min(size_x, size_y) >= BAND
            and mine_x % 128 == 0 and mine_y % 128 == 0 and n > 1)
    return kernel_form(n, *arrays) if fits else plain_form(*arrays)


def solution(mesh):
    in_specs = (
        P("groups", "gx", None),
        P("groups", "gx", None),
        P("groups", None, "gx"),
        P(),
        P(),
        P(),
        P(),
    )
    out_specs = (P("groups", None, "gx"), P("groups", "gx", None))
    return jax.shard_map(
        functools.partial(on_device, mesh.shape["gx"]),
        mesh=mesh, in_specs=in_specs, out_specs=out_specs, check_vma=False
    )
```

time: 786 us -> 391 us (0.50); the launches traced: 778 us -> 391 us
  Pallas kernels: 0 us -> 375 us
  matrix products: 338 us -> 0 us
  waiting for transfers between devices: 327 us -> 0 us
  other arithmetic: 49.2 us -> 2.15 us
  local copies, waits for them, and re-layouts: 50.1 us -> 12.4 us
  starting transfers between devices: 11.5 us -> 0 us
    pallas_call x0 -> x1, Pallas kernels: none -> 375 us  [kernel_form(): pl.pallas_call(functools.partial(fused, n), out_shape=(jax.ShapeDtypeStru...]
    dot_general x4 -> x0, matrix products: 338 us -> none  [the longest x2 183 us: smooth_x(): return jnp.einsum('ziy,ij->zjy', field, kernel_x, precision=high)]
    all_to_all x2 -> x0, waiting for transfers between devices: 327 us -> none  [the longest x1 170 us: on_device(): lax.all_to_all(back_x, 'gx', split_axis=1, concat_axis=2, tiled=True)]
    dot_general x4 -> x0, other arithmetic: 49.2 us -> none  [the longest x2 24.9 us: smooth_x(): return jnp.einsum('ziy,ij->zjy', field, kernel_x, precision=high)]
    all_to_all x3 -> x0, local copies, waits for them, and re-layouts: 30.2 us -> none  [the longest x2 20.9 us: on_device(): lax.all_to_all(back_x, 'gx', split_axis=1, concat_axis=2, tiled=True)]
    all_to_all x2 -> x0, starting transfers between devices: 11.5 us -> none  [the longest x1 6.56 us: on_device(): lax.all_to_all(along_y, 'gx', split_axis=2, concat_axis=1, tiled=True)]
    unnamed x10 -> x6, local copies, waits for them, and re-layouts: 0.02 us -> 11.1 us
    transpose x1 -> x0, local copies, waits for them, and re-layouts: 10.6 us -> none  [smooth_x(): return jnp.einsum('ziy,ij->zjy', field, kernel_x, precision=high)]
  transfers between devices with their start and end apart: 2 -> 0, of which waited for: 2 -> 0; matrix products, arithmetic and copies ran while one was open for 5% -> 0% of each run, Pallas kernels for 0% -> 0%
where the time goes in v1:
time: 391 us
  Pallas kernels  375 us (96%)
  local copies, waits for them, and re-layouts  12.4 us (3%)
    pallas_call x1, Pallas kernels, kernel_form(): pl.pallas_call(functools.partial(fused, n), out_shape=(jax.ShapeDtypeStru...  375 us
    unnamed x6, local copies, waits for them, and re-layouts  11.1 us

profile of v1, /device:TPU:13, one launch (start us, length us, event | category | flops | bytes accessed | tf_op | source)
XLA Modules:
  0.0 390.6 jit_solution(3440579826817448752)
XLA Ops:
  0.6 0.7 convert_element_type.6
  1.3 0.7 convert_element_type.7
  2.0 0.7 pad_maximum_fusion.rows
  2.8 0.0 copy-start.1
  2.8 1.3 copy.15
  4.1 0.0 copy-done.1
  4.1 375.4 %shard_map.86 = (f32[8,2048,128]{2,1,0:T(8,128)}, f32[8,128,2048]{2,1,0:T(8,128)}) custom-call(f32[8,128,2048]{2,1,0:T(8,128)} %cot.1, f32[8,128,2048]{2,1,0:T(8,128)} %sv.1, f32[8,2048,128]{2,1,0:T(8,128)} %su.1, f32[4,2048]{1,0:T(4,128)} %copy-done.1, f32[2048,4]{1,0:T(8,128)} %bitcast.5), custom_call_target="tpu_custom_call" | custom-call | flops 77309411328 | bytes 41943040 | tf_op jit(solution)/shard_map/pallas_call | solution.py:239
  379.5 0.0 copy-start
  379.5 7.7 %copy.18 = f32[8,2048,128]{2,1,0:T(8,128)} copy(f32[8,2048,128]{2,1,0:T(8,128)} %get-tuple-element.4) | data formatting | bytes 16777216
  387.2 0.0 copy-done
  387.2 3.4 copy.19
Async XLA Ops:
  2.8 1.4 copy-start.1
  379.5 7.7 %copy-start = (f32[8,128,2048]{2,1,0:T(8,128)S(1)}, f32[8,128,2048]{2,1,0:T(8,128)}, u32[]{:S(2)}) copy-start(f32[8,128,2048]{2,1,0:T(8,128)} %get-tuple-element.5) | copy-start | bytes 25165828

commit v2 on v1

--- a/solution.py
+++ b/solution.py
@@ -58,10 +58,10 @@
     return dot(a_hi, b_hi) + dot(a_hi, b_lo) + dot(a_lo, b_hi)
 
 
-def fused(n, cot, sv, su, rows, cols, gu, gv,
-          send_a, recv_a, send_b, recv_b, sv_buf, ky_hi, ky_lo, kx_hi, kx_lo,
+def fused(n, cot, sv, su, rows, cols, recv_a, send_a,
+          send_b, recv_b, sv_buf, ky_hi, ky_lo, kx_hi, kx_lo,
           wide_hi, wide_lo, tall_hi, tall_lo,
-          cot_sem, sv_sem, su_sem, gu_sem, gv_sem, sa_sem, ra_sem, sb_sem, rb_sem):
+          cot_sem, sv_sem, su_sem, sa_sem, ra_sem, sb_sem, rb_sem):
     count, mine_x, size_y = cot.shape
     size_x, mine_y = su.shape[1], su.shape[2]
     tiles_x, tiles_y = size_x // TILE, size_y // TILE
@@ -78,12 +78,6 @@
     def load_su(c):
         return pltpu.make_async_copy(su.at[c], send_b.at[c], su_sem.at[c])
 
-    def store_gu(c):
-        return pltpu.make_async_copy(recv_a.at[c], gu.at[c], gu_sem.at[c])
-
-    def store_gv(c):
-        return pltpu.make_async_copy(send_a.at[c], gv.at[c], gv_sem.at[c])
-
     for c in range(count):
         load_cot(c).start()
         if c < 2:
@@ -92,6 +86,14 @@
     barrier = pltpu.get_barrier_semaphore()
     for k in range(1, n):
         pl.semaphore_signal(barrier, inc=1, device_id={"gx": lax.rem(me + k, n)}, device_id_type=MESH)
+
+    def turn(s, tiles, mine):
+        half = tiles // 2
+        away = jnp.where(lax.rem(s, 2) == 0, half + s // 2, lax.rem((s + 1) // 2, half))
+        return lax.rem(my_tile(mine) + away, tiles)
+
+    def my_tile(mine):
+        return me // (TILE // mine)
 
     def band_start(t, size):
         return pl.multiple_of(jnp.clip(t * TILE - REACH, 0, size - BAND), TILE)
@@ -125,19 +127,15 @@
             kx_lo[t, :, s * TILE:(s + 1) * TILE] = lo
         return 0
 
-    def smooth_y(c):
-        def tile(t, _):
-            band = pl.ds(band_start(t, size_y), BAND)
-            send_a[c, :, pl.ds(pl.multiple_of(t * TILE, TILE), TILE)] = three(
-                wide_hi[:, band], wide_lo[:, band], ky_hi[t], ky_lo[t])
-            return 0
-        lax.fori_loop(0, tiles_y, tile, 0)
+    def smooth_y(c, t):
+        band = pl.ds(band_start(t, size_y), BAND)
+        send_a[c, :, pl.ds(pl.multiple_of(t * TILE, TILE), TILE)] = three(
+            wide_hi[:, band], wide_lo[:, band], ky_hi[t], ky_lo[t])
 
     def smooth_x(t):
         band = pl.ds(band_start(t, size_x), BAND)
         return three(kx_hi[t], kx_lo[t], tall_hi[band, :], tall_lo[band, :])
 
-    lax.fori_loop(0, tiles_y, build_y, 0)
     pl.semaphore_wait(barrier, n - 1)
 
     def first(c, _):
@@ -151,14 +149,27 @@
         def _():
             load_sv(c + 2).start()
 
-        smooth_y(c)
-        for k in range(1, n):
-            p = lax.rem(me + k, n)
-            pltpu.make_async_remote_copy(
-                src_ref=send_a.at[c, :, pl.ds(pl.multiple_of(p * mine_y, mine_y), mine_y)],
-                dst_ref=recv_a.at[c, pl.ds(my_x, mine_x), :],
-                send_sem=sa_sem.at[c], recv_sem=ra_sem.at[c],
-                device_id={"gx": p}, device_id_type=MESH).start()
+        def tile(s, _):
+            t = turn(s, tiles_y, mine_y)
+
+            @pl.when(c == 0)
+            def _():
+                build_y(t, 0)
+
+            smooth_y(c, t)
+            for k in range(TILE // mine_y):
+                p = t * (TILE // mine_y) + k
+
+                @pl.when(p != me)
+                def _():
+                    pltpu.make_async_remote_copy(
+                        src_ref=send_a.at[c, :, pl.ds(pl.multiple_of(p * mine_y, mine_y), mine_y)],
+                        dst_ref=recv_a.at[c, pl.ds(my_x, mine_x), :],
+                        send_sem=sa_sem.at[c], recv_sem=ra_sem.at[c],
+                        device_id={"gx": p}, device_id_type=MESH).start()
+            return 0
+
+        lax.fori_loop(0, tiles_y, tile, 0)
         recv_a[c, pl.ds(my_x, mine_x), :] = send_a[c, :, pl.ds(my_y, mine_y)]
         load_su(c).start()
         return 0
@@ -187,23 +198,26 @@
             return 0
 
         lax.fori_loop(0, tiles_x, up, 0)
-        store_gu(c).start()
         hi, lo = parts_of(recv_a[c])
         tall_hi[...] = hi
         tall_lo[...] = lo
 
-        def back(t, _):
+        def back(s, _):
+            t = turn(s, tiles_x, mine_x)
             send_b[c, pl.ds(pl.multiple_of(t * TILE, TILE), TILE), :] = smooth_x(t)
+            for k in range(TILE // mine_x):
+                p = t * (TILE // mine_x) + k
+
+                @pl.when(p != me)
+                def _():
+                    pltpu.make_async_remote_copy(
+                        src_ref=send_b.at[c, pl.ds(pl.multiple_of(p * mine_x, mine_x), mine_x), :],
+                        dst_ref=recv_b.at[c, :, pl.ds(my_y, mine_y)],
+                        send_sem=sb_sem.at[c], recv_sem=rb_sem.at[c],
+                        device_id={"gx": p}, device_id_type=MESH).start()
             return 0
 
         lax.fori_loop(0, tiles_x, back, 0)
-        for k in range(1, n):
-            p = lax.rem(me + k, n)
-            pltpu.make_async_remote_copy(
-                src_ref=send_b.at[c, pl.ds(pl.multiple_of(p * mine_x, mine_x), mine_x), :],
-                dst_ref=recv_b.at[c, :, pl.ds(my_y, mine_y)],
-                send_sem=sb_sem.at[c], recv_sem=rb_sem.at[c],
-                device_id={"gx": p}, device_id_type=MESH).start()
         recv_b[c, :, pl.ds(my_y, mine_y)] = send_b[c, pl.ds(my_x, mine_x), :]
         return 0
 
@@ -215,16 +229,18 @@
         hi, lo = parts_of(recv_b[c])
         wide_hi[...] = hi
         wide_lo[...] = lo
-        smooth_y(c)
-        store_gv(c).start()
+
+        def tile(t, _):
+            smooth_y(c, t)
+            return 0
+
+        lax.fori_loop(0, tiles_y, tile, 0)
         return 0
 
     lax.fori_loop(0, count, third, 0)
 
     def finish(c, _):
         tall_part(send_b, c, sb_sem).wait()
-        store_gu(c).wait()
-        store_gv(c).wait()
         return 0
 
     lax.fori_loop(0, count, finish, 0)
@@ -238,12 +254,10 @@
     work = 12 * 2 * count * BAND * (mine_x * size_y + mine_y * size_x)
     return pl.pallas_call(
         functools.partial(fused, n),
-        out_shape=(jax.ShapeDtypeStruct(saved_u.shape, f32), jax.ShapeDtypeStruct(cotangent.shape, f32)),
+        out_shape=(pltpu.VMEM(saved_u.shape, f32), pltpu.VMEM(cotangent.shape, f32)),
         in_specs=[pl.BlockSpec(memory_space=pl.ANY)] * 3 + [pl.BlockSpec(memory_space=pltpu.VMEM)] * 2,
-        out_specs=(pl.BlockSpec(memory_space=pl.ANY),) * 2,
+        out_specs=(pl.BlockSpec(memory_space=pltpu.VMEM),) * 2,
         scratch_shapes=[
-            pltpu.VMEM((count, mine_x, size_y), f32),
-            pltpu.VMEM((count, size_x, mine_y), f32),
             pltpu.VMEM((count, size_x, mine_y), f32),
             pltpu.VMEM((count, mine_x, size_y), f32),
             pltpu.VMEM((2, mine_x, size_y), f32),
@@ -255,9 +269,9 @@
             pltpu.VMEM((mine_x, size_y), bf16),
             pltpu.VMEM((size_x, mine_y), bf16),
             pltpu.VMEM((size_x, mine_y), bf16),
-        ] + [pltpu.SemaphoreType.DMA((count,))] * 9,
+        ] + [pltpu.SemaphoreType.DMA((count,))] * 7,
         compiler_params=pltpu.CompilerParams(
-            collective_id=0, has_side_effects=True, vmem_limit_bytes=60 * 2**20),
+            collective_id=0, has_side_effects=True, vmem_limit_bytes=44 * 2**20),
         cost_estimate=pl.CostEstimate(
             flops=work, bytes_accessed=20 * cotangent.size, transcendentals=0),
     )(cotangent, saved_v, saved_u, rows, rows.T)
@@ -265,8 +279,8 @@
 
 def on_device(n, *arrays):
     size_y, (size_x, mine_y), mine_x = arrays[0].shape[2], arrays[2].shape[1:], arrays[0].shape[1]
-    fits = (size_x % TILE == 0 and size_y % TILE == 0 and min(size_x, size_y) >= BAND
-            and mine_x % 128 == 0 and mine_y % 128 == 0 and n > 1)
+    fits = (size_x % (2 * TILE) == 0 and size_y % (2 * TILE) == 0 and min(size_x, size_y) >= BAND
+            and mine_x in (128, TILE) and mine_y in (128, TILE) and n > 1)
     return kernel_form(n, *arrays) if fits else plain_form(*arrays)
 
 

time: 391 us -> 385 us (0.985)
  local copies, waits for them, and re-layouts: 12.4 us -> 8.14 us
  Pallas kernels: 375 us -> 371 us
    pallas_call x1, Pallas kernels: 375 us -> 371 us  [kernel_form(): pl.pallas_call(functools.partial(fused, n), out_shape=(pltpu.VMEM(saved_u...]
    unnamed x6 -> x4, local copies, waits for them, and re-layouts: 11.1 us -> 6.8 us
where the time goes in v2:
time: 385 us; the launch traced here: 382 us
  Pallas kernels  371 us (96%)
  local copies, waits for them, and re-layouts  8.14 us (2%)
    pallas_call x1, Pallas kernels, kernel_form(): pl.pallas_call(functools.partial(fused, n), out_shape=(pltpu.VMEM(saved_u...  371 us

profile of v2, /device:TPU:13, one launch (start us, length us, event | category | flops | bytes accessed | tf_op | source)
XLA Modules:
  0.0 381.6 jit_solution(12433864943108675731)
XLA Ops:
  0.6 0.7 convert_element_type.6
  1.3 0.7 convert_element_type.7
  2.0 0.7 pad_maximum_fusion.rows
  2.8 0.0 copy-start
  2.8 1.3 copy.15
  4.1 0.0 copy-done
  4.1 370.7 %shard_map.86 = (f32[8,2048,128]{2,1,0:T(8,128)S(1)}, f32[8,128,2048]{2,1,0:T(8,128)S(1)}) custom-call(f32[8,128,2048]{2,1,0:T(8,128)} %cot.1, f32[8,128,2048]{2,1,0:T(8,128)} %sv.1, f32[8,2048,128]{2,1,0:T(8,128)} %su.1, f32[4,2048]{1,0:T(4,128)} %copy-done, f32[2048,4]{1,0:T(8,128)} %bitcast.5), custom_call_target="tpu_custom_call" | custom-call | flops 77309411328 | bytes 41943040 | tf_op jit(solution)/shard_map/pallas_call | solution.py:255
  374.9 3.4 copy.18
  378.3 3.4 copy.19
Async XLA Ops:
  2.8 1.4 copy-start

commit v3 on v2

--- a/solution.py
+++ b/solution.py
@@ -58,7 +58,7 @@
     return dot(a_hi, b_hi) + dot(a_hi, b_lo) + dot(a_lo, b_hi)
 
 
-def fused(n, cot, sv, su, rows, cols, recv_a, send_a,
+def fused(n, cot, sv, su, gain_x, width_x, gain_y, width_y, recv_a, send_a,
           send_b, recv_b, sv_buf, ky_hi, ky_lo, kx_hi, kx_lo,
           wide_hi, wide_lo, tall_hi, tall_lo,
           cot_sem, sv_sem, su_sem, sa_sem, ra_sem, sb_sem, rb_sem):
@@ -103,14 +103,19 @@
         cell = gain * jnp.exp(-offset * offset / (2.0 * SIGMA * SIGMA)) * SCALE
         return jnp.where(jnp.abs(offset) <= jnp.minimum(width_i, width_j), cell, 0.0)
 
+    def row(ref, at):
+        return ref[:, pl.ds(at, TILE)].astype(jnp.float32)
+
+    def column(ref, at):
+        return jnp.broadcast_to(row(ref, at), (128, TILE)).T[:, 0:1]
+
     def build_y(t, _):
         i0, j0 = band_start(t, size_y), pl.multiple_of(t * TILE, TILE)
         j = j0 + lax.broadcasted_iota(jnp.int32, (TILE, TILE), 1)
         for s in range(BAND // TILE):
             at = pl.multiple_of(i0 + s * TILE, TILE)
             i = at + lax.broadcasted_iota(jnp.int32, (TILE, TILE), 0)
-            hi, lo = parts_of(values(i, j, cols[pl.ds(at, TILE), 2:3], cols[pl.ds(at, TILE), 3:4],
-                                     rows[3:4, pl.ds(j0, TILE)]))
+            hi, lo = parts_of(values(i, j, column(gain_y, at), column(width_y, at), row(width_y, j0)))
             ky_hi[t, s * TILE:(s + 1) * TILE, :] = hi
             ky_lo[t, s * TILE:(s + 1) * TILE, :] = lo
         return 0
@@ -121,8 +126,7 @@
         for s in range(BAND // TILE):
             at = pl.multiple_of(i0 + s * TILE, TILE)
             i = at + lax.broadcasted_iota(jnp.int32, (TILE, TILE), 1)
-            hi, lo = parts_of(values(i, j, rows[0:1, pl.ds(at, TILE)], rows[1:2, pl.ds(at, TILE)],
-                                     cols[pl.ds(j0, TILE), 1:2]))
+            hi, lo = parts_of(values(i, j, row(gain_x, at), row(width_x, at), column(width_x, j0)))
             kx_hi[t, :, s * TILE:(s + 1) * TILE] = hi
             kx_lo[t, :, s * TILE:(s + 1) * TILE] = lo
         return 0
@@ -249,13 +253,13 @@
 def kernel_form(n, cotangent, saved_v, saved_u, gain_x, width_x, gain_y, width_y):
     count, mine_x, size_y = cotangent.shape
     size_x, mine_y = saved_u.shape[1:]
-    rows = jnp.stack([gain_x, width_x.astype(jnp.float32), gain_y, width_y.astype(jnp.float32)])
+    vectors = [v.reshape(1, -1) for v in (gain_x, width_x, gain_y, width_y)]
     f32, bf16 = jnp.float32, jnp.bfloat16
     work = 12 * 2 * count * BAND * (mine_x * size_y + mine_y * size_x)
     return pl.pallas_call(
         functools.partial(fused, n),
         out_shape=(pltpu.VMEM(saved_u.shape, f32), pltpu.VMEM(cotangent.shape, f32)),
-        in_specs=[pl.BlockSpec(memory_space=pl.ANY)] * 3 + [pl.BlockSpec(memory_space=pltpu.VMEM)] * 2,
+        in_specs=[pl.BlockSpec(memory_space=pl.ANY)] * 3 + [pl.BlockSpec(memory_space=pltpu.VMEM)] * 4,
         out_specs=(pl.BlockSpec(memory_space=pltpu.VMEM),) * 2,
         scratch_shapes=[
             pltpu.VMEM((count, size_x, mine_y), f32),
@@ -274,7 +278,7 @@
             collective_id=0, has_side_effects=True, vmem_limit_bytes=44 * 2**20),
         cost_estimate=pl.CostEstimate(
             flops=work, bytes_accessed=20 * cotangent.size, transcendentals=0),
-    )(cotangent, saved_v, saved_u, rows, rows.T)
+    )(cotangent, saved_v, saved_u, *vectors)
 
 
 def on_device(n, *arrays):

time: 385 us -> 381 us (0.990)
  no operation moved by 1% of the time
where the time goes in v3:
time: 381 us; the launch traced here: 378 us
  Pallas kernels  370 us (97%)
  local copies, waits for them, and re-layouts  6.8 us (2%)
    pallas_call x1, Pallas kernels, kernel_form(): pl.pallas_call(functools.partial(fused, n), out_shape=(pltpu.VMEM(saved_u...  370 us

profile of v3, /device:TPU:13, one launch (start us, length us, event | category | flops | bytes accessed | tf_op | source)
XLA Modules:
  0.0 377.9 jit_solution(11429251051318073861)
XLA Ops:
  0.6 370.4 %shard_map.86 = (f32[8,2048,128]{2,1,0:T(8,128)S(1)}, f32[8,128,2048]{2,1,0:T(8,128)S(1)}) custom-call(f32[8,128,2048]{2,1,0:T(8,128)} %cot.1, f32[8,128,2048]{2,1,0:T(8,128)} %sv.1, f32[8,2048,128]{2,1,0:T(8,128)} %su.1, f32[1,2048]{1,0:T(1,128)} %bitcast.4, s32[1,2048]{1,0:T(1,128)} %bitcast.5, f32[1,2048]{1,0:T(1,128)} %bitcast.6, s32[1,2048]{1,0:T(1,128)} %bitcast.7), custom_call_target="tpu_custom_call" | custom-call | flops 77309411328 | bytes 41943040 | tf_op jit(solution)/shard_map/pallas_call | solution.py:259
  371.1 3.4 copy.11
  374.5 3.4 copy.12
